TPU v7x, 256 devices: a whole 4x4x8 slice. The times are simulated.
256 devices in a mesh: ctx: 32 (over x, z), exp: 8 (over y, core).
Axes of the slice: x: 4, y: 4, z: 8, core: 2. Of those that a mesh axis runs over, the one named last changes fastest.
Arguments:
- queries: bfloat16 [1, 128, 48, 128], P(None, None, 'exp'), may hold values from -8 to 8
- new_kv: bfloat16 [1, 128, 2, 8, 128], P(None, 'ctx', None, 'exp'), may hold values from -8 to 8
- kv_cache: bfloat16 [2, 8, 512, 128, 128], P(None, 'exp', 'ctx'), may hold values from -8 to 8
- residual: bfloat16 [1, 128, 6144], P(None, 'ctx', 'exp'), may hold values from -4 to 4
- kept_blocks: int32 [2, 8, 128, 4], P(None, 'exp'), may hold values from -1 to 511, as said below
- block_moves: int32 [1, 8, 512], P(None, 'exp'), may hold values from 0 to 511, as said below
- expert_ids: int32 [1, 128, 2], replicated, may hold values from 0 to 7, all different within a row; in each aligned block of 4 rows (0 to 3, 4 to 7, ..., all dimensions but the last counted through in order) at most 2 rows name the same one
- gate_weights: float32 [1, 128, 2], replicated, may hold values from 0.2 to 1
- norm_gain: float32 [6144], replicated, may hold values from 0.1 to 1.9
- expert_in: bfloat16 [8, 2, 6144, 8192], P('exp', None, None, 'ctx'), may hold values from -0.078125 to 0.078125
- expert_out: bfloat16 [8, 8192, 6144], P('exp', 'ctx'), may hold values from -0.0625 to 0.0625
Outputs:
- layer_out: bfloat16 [1, 128, 6144], P(None, 'ctx', 'exp')
- final_cache: bfloat16 [2, 8, 512, 128, 128], P(None, 'exp', 'ctx')
Inputs may be any that keep to these rules, and one draw needn't show every extreme that they name: kept_blocks[s, h, b] lists slots of head h holding blocks of sequence b that step s attends; -1 marks an empty entry. A slot is listed at most once for a step and head. For each step and head, block_moves is a permutation of the 512 slots. The slots held by one index of ctx go to at most 1 slots of any one index of ctx, and to exactly 1 of some. `expert_ids`: each row names two different experts. Among the 4 tokens of one index of ctx (aligned blocks of 4 rows) no expert is named by more than 2 rows, and one is named by exactly 2.
All inputs are finite; a program needn't handle non-finite values.
Results may differ from a plain program's by a relative error of at most 0.013.
Values may be sent and summed in bfloat16 or wider, within the bound.
A program may use at most 128 MiB of HBM per device.

v0:
```python
import math

import jax
import jax.numpy as jnp
from jax import lax
from jax.sharding import PartitionSpec as P

NEG = -1e30
EPS = 1e-05


def combined_all(part, axis, combine):
    gathered = jax.tree.map(lambda a: lax.all_gather(a, axis), part)

    def take(source):
        return jax.tree.map(lambda a: lax.dynamic_index_in_dim(a, source, 0, False), gathered)

    return lax.fori_loop(
        1, lax.axis_size(axis), lambda source, state: combine(state, take(source)), take(0)
    )


def route_ranks(routing, expert_total):
    onehot = (routing[..., None] == jnp.arange(expert_total, dtype=jnp.int32)).astype(jnp.int32)
    per_token = jnp.sum(onehot, axis=-2)
    earlier = jnp.cumsum(per_token, axis=-2) - per_token
    return jnp.sum(onehot * earlier[..., None, :], axis=-1)


def join_partials(first, second):
    highest = jnp.maximum(first[0], second[0])
    left_scale = jnp.exp(first[0] - highest)
    right_scale = jnp.exp(second[0] - highest)
    return (
        highest,
        left_scale * first[1] + right_scale * second[1],
        left_scale[..., None] * first[2] + right_scale[..., None] * second[2],
    )


def per_device(
    queries,
    new_kv,
    kv_cache,
    residual,
    kept_blocks,
    block_moves,
    expert_ids,
    gate_weights,
    norm_gain,
    expert_in,
    expert_out,
):
    n_ctx = lax.axis_size("ctx")
    n_exp = lax.axis_size("exp")
    ctx_index = lax.axis_index("ctx")
    exp_index = lax.axis_index("exp")
    step_count, batch_rows, local_heads, head_dim = queries.shape
    group_count = kv_cache.shape[1]
    slot_count = kv_cache.shape[2]
    per_group = local_heads // group_count
    block_tokens = residual.shape[1]
    columns = residual.shape[2]
    local_experts = expert_in.shape[0]
    expert_total = local_experts * n_exp
    capacity = max(1, slot_count // n_ctx)
    expert_room = max(1, 4 * block_tokens // expert_total)
    scale = 1.0 / math.sqrt(head_dim)
    slot_ids = ctx_index * slot_count + jnp.arange(slot_count, dtype=jnp.int32)
    slot_range = jnp.arange(expert_room, dtype=jnp.int32)
    expert_range = jnp.arange(expert_total, dtype=jnp.int32)
    local_ids = exp_index * local_experts + jnp.arange(local_experts, dtype=jnp.int32)
    device_range = jnp.arange(n_ctx, dtype=jnp.int32)
    capacity_range = jnp.arange(capacity, dtype=jnp.int32)
    start_row = ctx_index * block_tokens
    cache = kv_cache
    listed = kept_blocks[0]
    owned = jnp.any(listed[..., None] == slot_ids, axis=2)
    queried = queries[0].reshape(batch_rows, group_count, per_group, head_dim)
    slot_query = jnp.einsum(
        "gbj,bgqd->jgqd", owned.astype(jnp.bfloat16), queried, preferred_element_type=jnp.float32
    ).astype(jnp.bfloat16)
    scores = (
        jnp.einsum("jgqd,gjrd->jgqr", slot_query, cache[0], preferred_element_type=jnp.float32)
        * scale
    )
    block_max = jnp.max(scores, axis=-1)
    probs = jnp.exp(scores - block_max[..., None]).astype(jnp.bfloat16)
    block_sum = jnp.sum(probs.astype(jnp.float32), axis=-1)
    block_out = jnp.einsum("jgqr,gjrd->jgqd", probs, cache[1], preferred_element_type=jnp.float32)
    member = jnp.transpose(owned, (1, 0, 2))[:, :, None, :]
    spread_max = jnp.transpose(block_max, (1, 2, 0))[None]
    seq_max = jnp.max(jnp.where(member, spread_max, NEG), axis=-1)
    factor = jnp.exp(jnp.where(member, spread_max - seq_max[..., None], NEG))
    seq_sum = jnp.einsum("bgqj,jgq->bgq", factor, block_sum, precision=lax.Precision.HIGHEST)
    seq_out = jnp.einsum("bgqj,jgqd->bgqd", factor, block_out, precision=lax.Precision.HIGHEST)
    merged = combined_all((seq_max, seq_sum, seq_out), "ctx", join_partials)
    highest = lax.dynamic_slice_in_dim(merged[0], start_row, block_tokens, 0)
    total = lax.dynamic_slice_in_dim(merged[1], start_row, block_tokens, 0)
    summed = lax.dynamic_slice_in_dim(merged[2], start_row, block_tokens, 0)
    own_query = lax.dynamic_slice_in_dim(queried, start_row, block_tokens, 0)
    own_score = (
        jnp.einsum("tgqd,tgd->tgq", own_query, new_kv[0, :, 0], preferred_element_type=jnp.float32)
        * scale
    )
    overall = jnp.maximum(highest, own_score)
    earlier = jnp.exp(highest - overall)
    fresh = jnp.exp(own_score - overall)
    denominator = earlier * total + fresh
    numerator = (
        earlier[..., None] * summed
        + fresh[..., None] * new_kv[0, :, 1].astype(jnp.float32)[:, :, None, :]
    )
    attention = (numerator / denominator[..., None]).reshape(block_tokens, columns)
    hidden_in = (residual[0].astype(jnp.float32) + attention).astype(jnp.bfloat16)
    route_all = expert_ids[0].reshape(n_ctx, block_tokens, 2)
    ranks_all = route_ranks(route_all, expert_total)
    gates_all = gate_weights[0].reshape(n_ctx, block_tokens, 2)
    routing = lax.dynamic_index_in_dim(route_all, ctx_index, 0, keepdims=False)
    ranking = lax.dynamic_index_in_dim(ranks_all, ctx_index, 0, keepdims=False)
    placing = (ranking[:, :, None, None] == slot_range[:, None]) & (
        routing[:, :, None, None] == expert_range
    )
    chosen = jnp.sum(placing.astype(jnp.float32), axis=1)
    packed = jnp.einsum(
        "trj,tc->rjc", chosen.astype(jnp.bfloat16), hidden_in, preferred_element_type=jnp.float32
    ).astype(jnp.bfloat16)
    packed = packed.reshape(expert_room, n_exp, local_experts, columns)
    arrived = lax.all_to_all(packed, "exp", split_axis=1, concat_axis=1, tiled=True)
    expert_rows = jnp.transpose(arrived, (0, 2, 1, 3)).reshape(
        expert_room, local_experts, n_exp * columns
    )
    wide = lax.all_gather(expert_rows, "ctx", axis=0, tiled=True).astype(jnp.float32)
    inverse = lax.rsqrt(jnp.mean(wide * wide, axis=-1, keepdims=True) + EPS)
    normed = (wide * inverse * norm_gain).astype(jnp.bfloat16)
    both = jnp.einsum("rld,lkdf->rlkf", normed, expert_in, preferred_element_type=jnp.float32)
    hidden = (jax.nn.silu(both[:, :, 0]) * both[:, :, 1]).astype(jnp.bfloat16)
    product = jnp.einsum("nlf,lfd->nld", hidden, expert_out, preferred_element_type=jnp.float32)
    product = product.reshape(n_ctx, expert_room, local_experts, n_exp * columns)
    picks = (ranks_all[..., None, None] == slot_range[:, None]) & (
        route_all[..., None, None] == local_ids
    )
    spread_gate = jnp.sum(jnp.where(picks, gates_all[..., None, None], 0.0), axis=2)
    term = jnp.einsum("ctrl,crld->ctd", spread_gate, product, precision=lax.Precision.HIGHEST)
    term = jnp.transpose(term.reshape(n_ctx, block_tokens, n_exp, columns), (0, 2, 1, 3))
    term = term.reshape(n_ctx * n_exp * block_tokens, columns)
    expert_sum = lax.psum_scatter(term, ("ctx", "exp"), scatter_dimension=0, tiled=True)
    outputs = [(hidden_in.astype(jnp.float32) + expert_sum).astype(jnp.bfloat16)]
    target_place = block_moves[0]
    target_dev = target_place // slot_count
    onehot_dev = (
        target_dev.reshape(group_count, n_ctx, slot_count)[..., None] == device_range
    ).astype(jnp.int32)
    rank_all = jnp.sum((jnp.cumsum(onehot_dev, axis=2) - onehot_dev) * onehot_dev, axis=-1)
    rank_all = rank_all.reshape(group_count, n_ctx * slot_count)
    my_dev = lax.dynamic_slice_in_dim(target_dev, ctx_index * slot_count, slot_count, 1)
    my_rank = lax.dynamic_slice_in_dim(rank_all, ctx_index * slot_count, slot_count, 1)
    sending = (my_dev[:, None, None, :] == device_range[:, None, None]) & (
        my_rank[:, None, None, :] == capacity_range[:, None]
    )
    outgoing = jnp.einsum(
        "gnmj,kgjrd->nmkgrd",
        sending.astype(jnp.bfloat16),
        cache,
        preferred_element_type=jnp.float32,
    ).astype(jnp.bfloat16)
    incoming = lax.all_to_all(outgoing, "ctx", split_axis=0, concat_axis=0, tiled=True)
    matching = target_place[:, None, :] == slot_ids[None, :, None]
    source = jnp.sum(
        jnp.where(matching, jnp.arange(n_ctx * slot_count, dtype=jnp.int32), 0), axis=-1
    )
    source_dev = source // slot_count
    source_rank = jnp.sum(jnp.where(matching, rank_all[:, None, :], 0), axis=-1)
    still_living = jnp.any(kept_blocks[1][..., None] == slot_ids, axis=(1, 2))
    taking = (
        (source_dev[..., None, None] == device_range[:, None])
        & (source_rank[..., None, None] == capacity_range)
        & still_living[..., None, None]
    )
    cache = jnp.einsum(
        "gqnm,nmkgrd->kgqrd",
        taking.astype(jnp.bfloat16),
        incoming,
        preferred_element_type=jnp.float32,
    ).astype(jnp.bfloat16)
    return (jnp.stack(outputs), cache)


def solution(mesh):
    in_specs = (
        P(None, None, "exp", None),
        P(None, "ctx", None, "exp", None),
        P(None, "exp", "ctx", None, None),
        P(None, "ctx", "exp"),
        P(None, "exp", None, None),
        P(None, "exp", None),
        P(),
        P(),
        P(),
        P("exp", None, None, "ctx"),
        P("exp", "ctx", None),
    )
    out_specs = (P(None, "ctx", "exp"), P(None, "exp", "ctx", None, None))
    return jax.shard_map(
        per_device, mesh=mesh, in_specs=in_specs, out_specs=out_specs, check_vma=False
    )
```

profile of v0, /device:TPU:1, one launch (start us, length us, event | category | flops | bytes accessed | tf_op | source)
XLA Modules:
  0.0 682.5 jit_solution(1717917522612083871)
XLA Ops:
  15.2 37.2 %all-gather.1 = f32[4096,1,6]{0,1,2:T(1,128)S(1)} all-gather(f32[128,1,6]{0,1,2:T(1,128)S(1)} %reshape_bitcast_fusion), channel_id=3, replica_groups=mesh['ctx'=32,'exp'=8] {'ctx'}, dimensions={0}, use_global_device_ids=true | all-gather | bytes 101376 | tf_op jit(solution)/shard_map/all_gather | solution.py:13
  53.0 32.6 %all-gather = f32[4096,6]{0,1:T(8,128)S(1)} all-gather(f32[128,6]{0,1:T(8,128)S(1)} %select_reduce_fusion), channel_id=2, replica_groups=mesh['ctx'=32,'exp'=8] {'ctx'}, dimensions={0}, use_global_device_ids=true | all-gather | bytes 101376 | tf_op jit(solution)/shard_map/all_gather | solution.py:13
  93.0 52.0 %all-gather.5.cloned.1.call-done = f32[4096,1,6,128]{0,3,2,1:T(8,128)} async-done(((f32[128,1,6,128]{0,3,2,1:T(8,128)}), f32[4096,1,6,128]{0,3,2,1:T(8,128)}) %all-gather.5.cloned.1.call-update) | async-done | bytes 12582928 | tf_op jit(solution)/shard_map/all_gather | solution.py:13
  147.0 15.6 %copy.157 = f32[4096,1,6,128]{3,2,0,1:T(8,128)} copy(f32[4096,1,6,128]{0,3,2,1:T(8,128)} %all-gather.5.cloned.1.call-done) | data formatting | bytes 25165824 | tf_op jit(solution)/shard_map/while | solution.py:18
  162.6 103.6 %while.19 = (s32[]{:T(128)}, f32[128,1,6]{0,1,2:T(1,128)S(1)}, f32[128,1,6]{0,1,2:T(1,128)S(1)}, f32[128,1,6,128]{3,2,1,0:T(8,128)}, f32[32,128,1,6]{1,0,3,2:T(8...) while((s32[]{:T(128)}, f32[128,1,6]{0,1,2:T(1,128)S(1)}, ...), condition=%wide.region_5.6_spmd, body=%wide.region_4.5_spmd.sunk | while | flops 299525 | bytes 1222807 | solution.py:18
  177.1 2.3 fusion.102
  180.4 2.3 fusion.102
  183.7 2.3 fusion.102
  187.1 2.3 fusion.102
  190.4 2.3 fusion.102
  193.8 2.3 fusion.102
  197.1 2.3 fusion.102
  257.3 2.3 fusion.102
  268.2 7.2 %all-to-all-start = ((bf16[2,8,1,768]{3,0,2,1:T(2,128)(2,1)}), bf16[2,8,1,768]{3,0,2,1:T(2,128)(2,1)S(1)}, u32[]{:S(2)}, u32[]{:S(2)}) async-start(bf16[2,8,1,768]{3,0,2,1:T(2,128)(2,1)} %copy.136), calls=%async_computation | async-start | bytes 49152 | tf_op jit(solution)/shard_map/all_to_all | solution.py:129
  280.1 6.0 all-to-all-start.1
  286.6 81.5 %all_gather.27 = bf16[64,1,6144]{2,1,0:T(2,128)(2,1)S(1)} all-gather(bf16[2,1,6144]{2,1,0:T(2,128)(2,1)S(1)} %copy.137), channel_id=1, replica_groups=mesh['ctx'=32,'exp'=8] {'ctx'}, dimensions={0}, use_global_device_ids=true | all-gather | bytes 811008 | tf_op jit(solution)/shard_map/all_gather | solution.py:133
  368.7 4.0 fusion.19
  374.5 3.1 reshape.852
  377.6 9.0 %fusion.93 = f32[32,4,6144]{2,1,0:T(4,128)} fusion(f32[32,4,2]{1,2,0:T(2,128)S(1)} %copy.139, f32[32,2,6144]{2,1,0:T(2,128)} %reshape.852), kind=kOutput, calls=%fused_computation.157 | convolution fusion | flops 18874368 | bytes 4719616 | tf_op jit(solution)/shard_map/ctrl,crld->ctd/dot_general | solution.py:144
  386.6 5.2 reshape.853
  391.8 4.8 copy.140
  396.6 4.9 reshape.854
  402.6 2.9 fusion.15
  406.7 267.6 %all-reduce.3.cloned.1.call-done = f32[1024,768]{1,0:T(8,128)} async-done(((f32[1024,768]{1,0:T(8,128)}), f32[1024,768]{1,0:T(8,128)}) %all-reduce.3.cloned.1.call-update) | async-done | bytes 3145744
  (234 shorter events, 115.7 us)
Async XLA Ops:
  7.2 365.5 %copy-start = (bf16[1,256,6144]{2,1,0:T(8,128)(2,1)S(1)}, bf16[1,256,6144]{2,1,0:T(8,128)(2,1)}, u32[]{:S(2)}) copy-start(bf16[1,256,6144]{2,1,0:T(8,128)(2,1)} %param.23) | copy-start | bytes 9437188
  7.2 79.1 %copy-start.17 = (s32[1,128,2]{1,2,0:T(2,128)S(1)}, s32[1,128,2]{1,2,0:T(2,128)}, u32[]{:S(2)}) copy-start(s32[1,128,2]{1,2,0:T(2,128)} %param.19) | copy-start | bytes 3076
  7.2 80.2 %copy-start.6 = (s32[1,1,512]{2,1,0:T(1,128)S(1)}, s32[1,1,512]{2,1,0:T(1,128)}, u32[]{:S(2)}) copy-start(s32[1,1,512]{2,1,0:T(1,128)} %param.18) | copy-start | bytes 6148
  7.2 84.5 %copy-start.16 = (bf16[1,4,2,1,128]{4,2,3,1,0:T(2,128)(2,1)S(1)}, bf16[1,4,2,1,128]{4,2,3,1,0:T(2,128)(2,1)}, u32[]{:S(2)}) copy-start(bf16[1,4,2,1,128]{4,2,3,1,0:T(2,128)(2,1)} %param.14) | copy-start | bytes 6148
  7.2 137.7 %all-gather.5.cloned.1.call-start = ((), (), s32[]{:S(2)}) async-start(), calls=%async_computation.2 | async-start | bytes 12976128 | tf_op jit(solution)/shard_map/all_gather | solution.py:13
  7.3 85.7 %copy-start.14 = (s32[16]{0:T(128)}, s32[16]{0:T(128)S(1)}, u32[]{:S(2)}) copy-start(s32[16]{0:T(128)S(1)} %iota_add_fusion) | copy-start | bytes 196
  52.4 0.6 copy-start.5
  86.4 6.5 copy-start.1
  88.8 4.1 copy-start.3
  162.6 103.9 %copy-start.13 = (f32[4,1,6]{2,1,0:T(1,128)S(1)}, f32[4,1,6]{2,1,0:T(1,128)}, u32[]{:S(2)}) copy-start(f32[4,1,6]{2,1,0:T(1,128)} %fusion.57) | copy-start | bytes 292
  162.6 103.9 %copy-start.9 = (f32[1,4,1,1,128]{4,2,3,1,0:T(1,128)S(1)}, f32[1,4,1,1,128]{4,2,3,1,0:T(1,128)}, u32[]{:S(2)}) copy-start(f32[1,4,1,1,128]{4,2,3,1,0:T(1,128)} %slice_convert_fusion) | copy-start | bytes 6148
  162.6 104.7 %copy-start.10 = (bf16[1,4,768]{2,1,0:T(4,128)(2,1)S(1)}, bf16[1,4,768]{2,1,0:T(4,128)(2,1)}, u32[]{:S(2)}) copy-start(bf16[1,4,768]{2,1,0:T(4,128)(2,1)} %param.16) | copy-start | bytes 18436
  162.6 104.8 %copy-start.8 = (bf16[4,2,8]{2,0,1:T(4,128)(2,1)S(1)}, bf16[4,2,8]{2,0,1:T(4,128)(2,1)}, u32[]{:S(2)}) copy-start(bf16[4,2,8]{2,0,1:T(4,128)(2,1)} %convert_reduce_fusion.2) | copy-start | bytes 388
  162.6 112.7 %copy-start.12 = (s32[16]{0:T(128)S(1)}, s32[16]{0:T(128)}, u32[]{:S(2)}) copy-start(s32[16]{0:T(128)} %fusion.84) | copy-start | bytes 196
  162.6 112.7 %copy-start.19 = (pred[16]{0:T(512)(128)(4,1)S(1)}, pred[16]{0:T(512)(128)(4,1)}, u32[]{:S(2)}) copy-start(pred[16]{0:T(512)(128)(4,1)} %compare_bitcast_fusion) | copy-start | bytes 52
  268.2 11.8 %all-to-all-start = ((bf16[2,8,1,768]{3,0,2,1:T(2,128)(2,1)}), bf16[2,8,1,768]{3,0,2,1:T(2,128)(2,1)S(1)}, u32[]{:S(2)}, u32[]{:S(2)}) async-start(bf16[2,8,1,768]{3,0,2,1:T(2,128)(2,1)} %copy.136), calls=%async_computation | async-start | bytes 49152 | tf_op jit(solution)/shard_map/all_to_all | solution.py:129
  279.9 6.3 copy-start.2
  279.9 6.4 copy-start.18
  280.1 122.5 %all-to-all-start.1 = ((bf16[32,1,2,1,128,128]{5,4,2,1,3,0:T(8,128)(2,1)}), bf16[32,1,2,1,128,128]{5,4,2,1,3,0:T(8,128)(2,1)}, u32[]{:S(2)}, u32[]{:S(2)}) async-start(bf16[32,1,2,1,128,128]{5,4,2,1,3,0:T(8,128)(2,1)} %copy.144), calls=%async_computation.1 | async-start | bytes 4194304 | tf_op jit(solution)/shard_map/all_to_all | solution.py:167
  286.1 82.6 %copy-start.7 = (f32[6144]{0:T(1024)S(1)}, f32[6144]{0:T(1024)}, u32[]{:S(2)}) copy-start(f32[6144]{0:T(1024)} %param.21) | copy-start | bytes 73732
  286.1 388.2 %all-reduce.3.cloned.1.call-start = ((), (), s32[]{:S(2)}) async-start(), calls=%async_computation.3 | async-start | bytes 6291456
  401.5 0.7 copy-start.4
  401.5 0.8 copy-start.15
  401.5 1.0 copy-start.11
Sparse Core Ops, SparseCore 0:
  14.8 130.1 all-gather.4
  401.7 272.5 all-reduce.2
where the time goes:
time: 687 us; the launch traced here: 682 us
  waiting for transfers between devices  320 us (47%)
  blocking collectives  151 us (22%)
  other arithmetic  105 us (15%)
  local copies, waits for them, and re-layouts  52.5 us (8%)
  matrix products  26.6 us (4%)
  between operations  14.4 us (2%)
  starting transfers between devices  13.2 us (2%)
    unnamed x3, waiting for transfers between devices  268 us
    all_gather x1, blocking collectives, per_device(): lax.all_gather(expert_rows, 'ctx', axis=0, tiled=True).astype(jnp.float32)  81.5 us
    add x31, other arithmetic, join_partials(): left_scale[..., None] * first[2] + right_scale[..., None] * second[2]  72.3 us
    all_gather x2, blocking collectives, combined_all(): gathered = jax.tree.map(lambda a: lax.all_gather(a, axis), part)  69.8 us
    all_gather x1, waiting for transfers between devices, combined_all(): gathered = jax.tree.map(lambda a: lax.all_gather(a, axis), part)  52 us
    add x31, other arithmetic, join_partials(): left_scale * first[1] + right_scale * second[1]  24.3 us
    while x5, local copies, waits for them, and re-layouts, combined_all(): lax.fori_loop(1, lax.axis_size(axis), lambda source, state: combine(state...  16.9 us
  transfers between devices with their start and end apart: 4, of which 3 were waited for; matrix products, arithmetic and copies ran while one was open for 7% of the time, Pallas kernels for 0%

commit v1 on v0

v1 whole, which is shorter than its diff:
```python
import functools
import math

import jax
import jax.numpy as jnp
from jax import lax
from jax.experimental import pallas as pl
from jax.experimental.pallas import tpu as pltpu
from jax.sharding import PartitionSpec as P

MESH = pl.DeviceIdType.MESH
NEG = -1e30
EPS = 1e-05
F32, BF16, I32 = jnp.float32, jnp.bfloat16, jnp.int32

DZ_ORDER = (4, 3, 5, 2, 6, 1, 7, 0)
ORDER = tuple((dx, dz) for dz in DZ_ORDER for dx in (2, 1, 3, 0) if (dx, dz) != (0, 0))
PACE = (0, 4, 4, 4, 8, 8, 3, 0)


def iota(shape, dim):
    return lax.broadcasted_iota(I32, shape, dim)


def dot(a, b):
    return jnp.dot(a, b, preferred_element_type=F32)


def dot_nt(a, b):
    return lax.dot_general(a, b, (((1,), (1,)), ((), ())), preferred_element_type=F32)


def split3(v):
    first = v.astype(BF16).astype(F32)
    second = (v - first).astype(BF16).astype(F32)
    return first, second, v - first - second


def kernel(
    moves_hbm, kept_hbm, cache_hbm, q_hbm, nkv_hbm, res_hbm, ids_hbm, gates_hbm, gain_hbm, win_hbm, wout_hbm,
    lay_ref, fin_ref,
    moves_ref, kept_ref, cache, q_ref, nkv_ref, res_ref, ids_ref, gates_ref, gain_ref, win, wout, idxv, idxs, send_a, recv_a, gx, send_e, recv_e, send_f, recv_f, send_g, recv_g, send_h, recv_h,
    send_r, recv_r, scr, nks, nvs, slots, gatev, selt, att_s, res_s,
    lsem, sa, ra, sc, rc, sd, rd, se, re, sf, rf, sg, rg, sh, rh, sr, rr,
):
    c = lax.axis_index("ctx")
    e = lax.axis_index("exp")
    x, z = lax.div(c, 8), lax.rem(c, 8)
    y, k = lax.div(e, 2), lax.rem(e, 2)
    scale = 1.0 / math.sqrt(128)

    def ctx_at(dx, dz):
        return lax.rem(x + dx, 4) * 8 + lax.rem(z + dz, 8)

    def exp_at(dy, dk):
        return lax.rem(y + dy, 4) * 2 + lax.rem(k + dk, 2)

    def remote(src, dst, s, r, ctx=None, exp=None):
        return pltpu.make_async_remote_copy(
            src_ref=src, dst_ref=dst, send_sem=s, recv_sem=r,
            device_id=(c if ctx is None else ctx, e if exp is None else exp), device_id_type=MESH,
        )

    sources = (moves_hbm, kept_hbm, cache_hbm, q_hbm, nkv_hbm, res_hbm, ids_hbm, gates_hbm, gain_hbm, win_hbm, wout_hbm)
    targets = (moves_ref, kept_ref, cache, q_ref, nkv_ref, res_ref, ids_ref, gates_ref, gain_ref, win, wout)
    loads = [pltpu.make_async_copy(a, b, lsem.at[i]) for i, (a, b) in enumerate(zip(sources, targets))]
    for load in loads[:9]:
        load.start()

    barrier = pltpu.get_barrier_semaphore()

    def greet_ctx(o, carry):
        pl.semaphore_signal(
            barrier, inc=1, device_id=(ctx_at(lax.div(o, 8), lax.rem(o, 8)), e), device_id_type=MESH
        )
        return carry

    def greet_exp(o, carry):
        pl.semaphore_signal(
            barrier, inc=1, device_id=(c, exp_at(lax.div(o, 2), lax.rem(o, 2))), device_id_type=MESH
        )
        return carry

    lax.fori_loop(1, 32, greet_ctx, 0)
    lax.fori_loop(1, 8, greet_exp, 0)

    loads[0].wait()
    loads[1].wait()
    mv = moves_ref[...]
    lane = iota((32, 512), 1)
    off = iota((32, 512), 0)
    target = ((x + (off >> 3)) & 3) * 8 + ((z + (off & 7)) & 7)
    hit = ((mv >> 4) == target) & ((lane >> 4) == c)
    srcj = jnp.max(jnp.where(hit, lane & 15, 0), axis=1, keepdims=True)
    lane = iota((16, 512), 1)
    hit = mv == 16 * c + iota((16, 512), 0)
    place = ((x - (lane >> 7)) & 3) * 8 + ((z - ((lane >> 4) & 7)) & 7)
    rslot = jnp.max(jnp.where(hit, place, 0), axis=1, keepdims=True)
    kept1 = kept_ref[1]
    slot16 = 16 * c + iota((16, 128), 0)
    alive = kept1[0:1] == slot16
    for j in range(1, 4):
        alive = alive | (kept1[j : j + 1] == slot16)
    living = jnp.max(jnp.where(alive, 1, 0), axis=1, keepdims=True)
    eye32 = iota((32, 128), 0) == iota((32, 128), 1)
    eye16 = iota((16, 128), 0) == iota((16, 128), 1)
    idxv[0:1, :] = jnp.sum(jnp.where(eye32, srcj, 0), axis=0, keepdims=True)
    idxv[1:2, :] = jnp.sum(jnp.where(eye16, rslot, 0), axis=0, keepdims=True)
    idxv[2:3, :] = jnp.sum(jnp.where(eye16, living, 0), axis=0, keepdims=True)
    to_smem = pltpu.make_async_copy(idxv, idxs, lsem.at[11])
    to_smem.start()

    loads[2].wait()
    loads[9].start()
    loads[10].start()
    to_smem.wait()

    def pack(o, carry):
        send_r[o] = cache[:, idxs[0, o]]
        return carry

    lax.fori_loop(0, 32, pack, 0)

    pl.semaphore_wait(barrier, 38)

    def copy_a(o):
        dx, dz = lax.div(o, 8), lax.rem(o, 8)
        t = ctx_at(dx, dz)
        return remote(send_a.at[t], recv_a.at[o], sa.at[o], ra.at[o], ctx=t)

    def copy_r(o, dx, dz):
        return remote(send_r.at[o], recv_r.at[o], sr.at[o], rr.at[o], ctx=ctx_at(dx, dz))

    done = [0]

    def relocate(count):
        for dx, dz in ORDER[done[0] : done[0] + count]:
            copy_r(dx * 8 + dz, dx, dz).start()
        done[0] += count

    def loop(lo, hi, body):
        def step(o, carry):
            body(o)
            return carry

        lax.fori_loop(lo, hi, step, 0)

    relocate(PACE[0])

    rsub, rlane = iota((128, 128), 0), iota((128, 128), 1)
    kept0 = kept_ref[0]
    slot_id = 16 * c + (rsub & 15)
    owned = kept0[0:1] == slot_id
    for j in range(1, 4):
        owned = owned | (kept0[j : j + 1] == slot_id)
    owned = owned & (rsub < 96)
    ownf = jnp.where(owned, 1.0, 0.0)
    ownb = ownf.astype(BF16)
    owncol = jnp.sum(jnp.where(owned, rlane, 0), axis=1, keepdims=True)
    ownrow = dot_nt(iota((8, 128), 1).astype(F32).astype(BF16), ownb)[0:1].astype(I32)
    loads[3].wait()
    heads = [dot(ownb[16 * i : 16 * i + 16], q_ref[i]) for i in range(6)]
    q96 = jnp.concatenate(heads + [jnp.zeros((32, 128), F32)], axis=0).astype(BF16)
    scores = jnp.zeros((128, 128), F32)
    for j in range(16):
        scores = jnp.where((rsub & 15) == j, dot_nt(q96, cache[0, j]), scores)
    scores = scores * scale
    m = jnp.max(scores, axis=1, keepdims=True)
    probs = jnp.exp(scores - m).astype(BF16)
    l = jnp.sum(probs.astype(F32), axis=1, keepdims=True)
    out = jnp.zeros((128, 128), F32)
    for j in range(16):
        out = jnp.where((rsub & 15) == j, dot(probs, cache[1, j]), out)
    eye = rsub == rlane
    same = (owncol == ownrow) & ((rsub >> 4) == (rlane >> 4))
    mrow = jnp.sum(jnp.where(eye, m, 0.0), axis=0, keepdims=True)
    mseq = jnp.max(jnp.where(same, mrow, NEG), axis=1, keepdims=True)
    f = jnp.exp(m - mseq)
    lrow = jnp.sum(jnp.where(eye, l * f, 0.0), axis=0, keepdims=True)
    lseq = jnp.sum(jnp.where(same, lrow, 0.0), axis=1, keepdims=True)
    first = jnp.min(jnp.where(same, rlane.astype(F32), 999.0), axis=1, keepdims=True)
    place = ((rsub >> 4) << 2) + (owncol & 3)
    spread = (place == rlane) & (first == rsub.astype(F32)) & (rsub < 96)
    stats = [jnp.where(spread, v, 0.0).astype(BF16) for v in split3(mseq) + split3(lseq)]
    rl = iota((1, 128), 1)
    code = jnp.where(rl < 96, ((ownrow >> 2) << 5) + ((rl >> 4) << 2) + (ownrow & 3), -1)
    lift = jnp.where(iota((1024, 128), 0) == code, 1.0, 0.0).astype(BF16)
    values = dot(lift, (out * f).astype(BF16)).reshape(32, 32, 128)
    code = jnp.where(rl < 96, (ownrow >> 2) << 3, -100)
    row256 = iota((256, 128), 0)
    lift = jnp.concatenate([jnp.where(row256 == code + t, 1.0, 0.0).astype(BF16) for t in range(6)], axis=1)
    stat = dot(lift, jnp.concatenate(stats, axis=0)).reshape(32, 8, 128)
    send_a[...] = jnp.concatenate([values[:, 0:24], stat], axis=1).astype(BF16)

    loop(1, 32, lambda o: copy_a(o).start())
    relocate(PACE[1])
    recv_a[0] = send_a[c]

    for load in loads[4:9]:
        load.wait()
    res = res_ref[...].astype(F32)
    nks[0:4] = nkv_ref[:, 0].astype(F32)
    nks[4:8] = nkv_ref[:, 0].astype(F32)
    nvs[0:4] = nkv_ref[:, 1].astype(F32)
    nvs[4:8] = nkv_ref[:, 1].astype(F32)
    for i in range(6):
        res_s[4 * i : 4 * i + 4] = res[:, 128 * i : 128 * i + 128]
    s8, b8 = iota((8, 128), 0), iota((8, 128), 1)
    low = jnp.where((s8 < 4) & (b8 == 4 * c + s8), 1.0, 0.0).astype(BF16)
    high = jnp.where((s8 >= 4) & (b8 == 4 * c + s8 - 4), 1.0, 0.0).astype(BF16)
    q24 = jnp.concatenate([dot(low, q_ref[2 * p]) + dot(high, q_ref[2 * p + 1]) for p in range(3)], axis=0)
    nk24 = jnp.concatenate([nks[...]] * 3, axis=0)
    nv24 = jnp.concatenate([nvs[...]] * 3, axis=0)
    own_score = jnp.sum(q24 * nk24, axis=1, keepdims=True) * scale
    eye24 = iota((24, 128), 0) == iota((24, 128), 1)
    own_score = jnp.sum(jnp.where(eye24, own_score, 0.0), axis=0, keepdims=True)

    g3 = split3(gates_ref[...])
    scr[0:2] = ids_ref[...].astype(F32)
    for i in range(3):
        scr[2 * i + 2 : 2 * i + 4] = g3[i]
    o128 = rlane >> 2
    group = ((x - (o128 >> 3)) & 3) * 8 + ((z - (o128 & 7)) & 7)
    relative = jnp.where(rsub == 4 * group + (rlane & 3), 1.0, 0.0).astype(BF16)
    routed = dot(scr[...].astype(BF16), relative)
    r0, r1 = routed[0:1].astype(I32), routed[1:2].astype(I32)
    w0 = routed[2:3] + routed[4:5] + routed[6:7]
    w1 = routed[3:4] + routed[5:6] + routed[7:8]
    goes = jnp.where((r0 == s8) | (r1 == s8), 1, 0)
    rank = jnp.zeros((8, 128), I32)
    for d in range(1, 4):
        rank = rank + jnp.where((b8 & 3) >= d, pltpu.roll(goes, d, 1), 0)
    slot = jnp.where(goes > 0, ((b8 >> 2) << 1) + rank, -1)
    slots[...] = slot
    gatev[...] = jnp.where(r0 == s8, w0, 0.0) + jnp.where(r1 == s8, w1, 0.0)
    row64 = iota((64, 128), 0)
    sel = jnp.concatenate([jnp.where(row64 == slot[j : j + 1], 1.0, 0.0) for j in range(8)], axis=0)
    selt[...] = sel.T.astype(BF16)
    sel = sel.astype(BF16)
    gate_col = jnp.sum(
        jnp.where(row64 == slots[pl.ds(e, 1)], gatev[pl.ds(e, 1)], 0.0), axis=1, keepdims=True
    )

    loop(1, 32, lambda o: copy_a(o).wait_recv())
    got = recv_a[...].astype(F32)
    st = got[:, 24:32]
    qi = iota((32, 8, 128), 1)
    m = jnp.sum(jnp.where(qi < 3, st, 0.0), axis=1, keepdims=True)
    l = jnp.sum(jnp.where((qi >= 3) & (qi < 6), st, 0.0), axis=1, keepdims=True)
    m = jnp.where(l > 0, m, NEG)
    top = jnp.maximum(jnp.max(m, axis=0), own_score)
    w = jnp.where(l > 0, jnp.exp(m - top[None]), 0.0)
    fresh = jnp.exp(own_score - top)
    inv_den = 1.0 / (jnp.sum(w * l, axis=0) + fresh)
    w = w * inv_den[None]
    wcol = jnp.sum(jnp.where(eye24[None], jnp.broadcast_to(w, (32, 24, 128)), 0.0), axis=2, keepdims=True)
    att = jnp.sum(wcol * got[:, 0:24], axis=0)
    fcol = jnp.sum(jnp.where(eye24, fresh * inv_den, 0.0), axis=1, keepdims=True)
    att = att + fcol * nv24
    hidden = (res_s[...] + att).astype(BF16).astype(F32)
    gx[0, 0] = jnp.concatenate([hidden, jnp.zeros((8, 128), F32)], axis=0).astype(BF16)

    def copy_c(dz):
        return remote(gx.at[0, 0], gx.at[0, dz], sc.at[dz], rc.at[dz], ctx=ctx_at(0, dz))

    def copy_d(dx):
        return remote(gx.at[0], gx.at[dx], sd.at[dx], rd.at[dx], ctx=ctx_at(dx, 0))

    loop(1, 8, lambda dz: copy_c(dz).start())
    relocate(PACE[2])
    loop(1, 8, lambda dz: copy_c(dz).wait_recv())
    loop(1, 4, lambda dx: copy_d(dx).start())
    relocate(PACE[3])
    loop(1, 4, lambda dx: copy_d(dx).wait_recv())

    flat = gx[...].reshape(32, 32, 128).astype(F32).reshape(16, 2, 32, 128)
    sub16 = iota((16, 8, 128), 1)
    parts = []
    for p in range(3):
        one, two = flat[:, 0, 8 * p : 8 * p + 8], flat[:, 1, 8 * p : 8 * p + 8]
        parts.append(jnp.where(sub16 < 4, one, pltpu.roll(two, 4, 1)).reshape(128, 128).astype(BF16))
        parts.append(jnp.where(sub16 < 4, pltpu.roll(one, 4, 1), two).reshape(128, 128).astype(BF16))
    tokens = jnp.concatenate(parts, axis=1)

    def copy_e(o):
        t = exp_at(lax.div(o, 2), lax.rem(o, 2))
        return remote(send_e.at[t], recv_e.at[e], se.at[o], re.at[o], exp=t)

    for j in range(8):
        send_e[j] = dot(sel[64 * j : 64 * j + 64], tokens).astype(BF16)
    loop(1, 8, lambda o: copy_e(o).start())
    relocate(PACE[4])
    recv_e[e] = send_e[e]
    loads[9].wait()

    def first_half(o, carry):
        gate, upper, square = carry
        src = lax.rem(y + 4 - lax.div(o, 2), 4) * 2 + lax.rem(k + lax.rem(o, 2), 2)
        rows = recv_e[src].astype(F32)
        square = square + jnp.sum(rows * rows, axis=1, keepdims=True)
        gain = jnp.concatenate([gain_ref[pl.ds(6 * src + i, 1)] for i in range(6)], axis=1)
        scaled = (rows * gain).astype(BF16)
        start = pl.multiple_of(src * 768, 768)
        gate = gate + dot(scaled, win[0, pl.ds(start, 768)])
        upper = upper + dot(scaled, win[1, pl.ds(start, 768)])
        return gate, upper, square

    def arrived(o, carry):
        copy_e(o).wait_recv()
        return first_half(o, carry)

    zero = jnp.zeros((64, 256), F32)
    carry = first_half(0, (zero, zero, jnp.zeros((64, 1), F32)))
    gate, upper, square = lax.fori_loop(1, 8, arrived, carry)
    inverse = lax.rsqrt(square * (1.0 / 6144) + EPS)
    gate = gate * inverse
    act = (gate / (1.0 + jnp.exp(-gate)) * (upper * inverse)).astype(BF16)
    loads[10].wait()

    def copy_f(o):
        t = exp_at(lax.div(o, 2), lax.rem(o, 2))
        return remote(send_f.at[t], recv_f.at[e], sf.at[o], rf.at[o], exp=t)

    def second_half(t):
        start = pl.multiple_of(t * 768, 768)
        return (dot(act, wout[:, pl.ds(start, 768)]) * gate_col).astype(BF16)

    def produce(n):
        o = 8 - n
        t = exp_at(lax.div(o, 2), lax.rem(o, 2))
        send_f[t] = second_half(t)
        copy_f(o).start()

    loop(1, 8, produce)
    relocate(PACE[5])
    recv_f[e] = second_half(e)
    loop(1, 8, lambda o: copy_f(o).wait_recv())
    mixed = dot(selt[...], recv_f[...].reshape(512, 768))
    for dx in range(1, 4):
        send_g[dx] = mixed[32 * dx : 32 * dx + 32].astype(BF16)

    def copy_g(dx):
        return remote(send_g.at[dx], recv_g.at[dx], sg.at[dx], rg.at[dx], ctx=ctx_at(4 - dx, 0))

    def copy_h(dz):
        return remote(send_h.at[dz], recv_h.at[dz], sh.at[dz], rh.at[dz], ctx=ctx_at(0, 8 - dz))

    loop(1, 4, lambda dx: copy_g(dx).start())
    relocate(PACE[6])
    loop(1, 4, lambda dx: copy_g(dx).wait_recv())
    summed = mixed[0:32] + recv_g[1].astype(F32) + recv_g[2].astype(F32) + recv_g[3].astype(F32)
    cols = [summed[:, 128 * i : 128 * i + 128].reshape(4, 8, 128) for i in range(6)]
    sub4 = iota((4, 8, 128), 1)
    evens, odds = [], []
    for p in range(3):
        one, two = cols[2 * p], cols[2 * p + 1]
        evens.append(jnp.where(sub4 < 4, one, pltpu.roll(two, 4, 1)))
        odds.append(jnp.where(sub4 < 4, pltpu.roll(one, 4, 1), two))
    pad = [jnp.zeros((4, 8, 128), F32)]
    evens, odds = jnp.concatenate(evens + pad, axis=1), jnp.concatenate(odds + pad, axis=1)
    for n in range(4):
        send_h[2 * n] = evens[n].astype(BF16)
        send_h[2 * n + 1] = odds[n].astype(BF16)
    loop(1, 8, lambda dz: copy_h(dz).start())
    relocate(31)

    loop(1, 8, lambda dz: copy_h(dz).wait_recv())
    total = hidden + evens[0, 0:24]
    for dz in range(1, 8):
        total = total + recv_h[dz].astype(F32)[0:24]
    att_s[...] = total
    for i in range(6):
        lay_ref[:, 128 * i : 128 * i + 128] = att_s[4 * i : 4 * i + 4].astype(BF16)

    recv_r[0] = send_r[0]
    loop(1, 32, lambda o: copy_r(o, lax.div(o, 8), lax.rem(o, 8)).wait_recv())

    def place_block(s):
        block = recv_r[idxs[1, s]]
        fin_ref[:, s] = jnp.where(idxs[2, s] > 0, block, jnp.zeros_like(block))

    loop(0, 16, place_block)

    loop(1, 32, lambda o: copy_a(o).wait_send())
    loop(1, 8, lambda dz: copy_c(dz).wait_send())
    loop(1, 4, lambda dx: copy_d(dx).wait_send())
    loop(1, 8, lambda o: copy_e(o).wait_send())
    loop(1, 8, lambda o: copy_f(o).wait_send())
    loop(1, 4, lambda dx: copy_g(dx).wait_send())
    loop(1, 8, lambda dz: copy_h(dz).wait_send())
    loop(1, 32, lambda o: copy_r(o, lax.div(o, 8), lax.rem(o, 8)).wait_send())


def per_device(
    queries, new_kv, kv_cache, residual, kept_blocks, block_moves, expert_ids, gate_weights, norm_gain, expert_in,
    expert_out,
):
    vmem = pl.BlockSpec(memory_space=pltpu.VMEM)
    hbm = pl.BlockSpec(memory_space=pl.ANY)
    dma = pltpu.SemaphoreType.DMA
    layer, final = pl.pallas_call(
        kernel,
        out_shape=(
            jax.ShapeDtypeStruct((4, 768), BF16),
            jax.ShapeDtypeStruct((2, 16, 128, 128), BF16),
        ),
        in_specs=[hbm] * 11,
        out_specs=(vmem, vmem),
        scratch_shapes=[
            pltpu.VMEM((1, 512), I32),
            pltpu.VMEM((2, 4, 128), I32),
            pltpu.VMEM((2, 16, 128, 128), BF16),
            pltpu.VMEM((6, 128, 128), BF16),
            pltpu.VMEM((4, 2, 128), BF16),
            pltpu.VMEM((4, 768), BF16),
            pltpu.VMEM((2, 128), I32),
            pltpu.VMEM((2, 128), F32),
            pltpu.VMEM((48, 128), F32),
            pltpu.VMEM((2, 6144, 256), BF16),
            pltpu.VMEM((256, 6144), BF16),
            pltpu.VMEM((8, 128), I32),
            pltpu.SMEM((8, 128), I32),
            pltpu.VMEM((32, 32, 128), BF16),
            pltpu.VMEM((32, 32, 128), BF16),
            pltpu.VMEM((4, 8, 32, 128), BF16),
            pltpu.VMEM((8, 64, 768), BF16),
            pltpu.VMEM((8, 64, 768), BF16),
            pltpu.VMEM((8, 64, 768), BF16),
            pltpu.VMEM((8, 64, 768), BF16),
            pltpu.VMEM((4, 32, 768), BF16),
            pltpu.VMEM((4, 32, 768), BF16),
            pltpu.VMEM((8, 32, 128), BF16),
            pltpu.VMEM((8, 32, 128), BF16),
            pltpu.VMEM((32, 2, 128, 128), BF16),
            pltpu.VMEM((32, 2, 128, 128), BF16),
            pltpu.VMEM((8, 128), F32),
            pltpu.VMEM((8, 128), F32),
            pltpu.VMEM((8, 128), F32),
            pltpu.VMEM((8, 128), I32),
            pltpu.VMEM((8, 128), F32),
            pltpu.VMEM((128, 512), BF16),
            pltpu.VMEM((24, 128), F32),
            pltpu.VMEM((24, 128), F32),
            dma((12,)),
            dma((32,)), dma((32,)),
            dma((8,)), dma((8,)),
            dma((4,)), dma((4,)),
            dma((8,)), dma((8,)),
            dma((8,)), dma((8,)),
            dma((4,)), dma((4,)),
            dma((8,)), dma((8,)),
            dma((32,)), dma((32,)),
        ],
        compiler_params=pltpu.CompilerParams(
            collective_id=0, has_side_effects=True, vmem_limit_bytes=60 * 1024 * 1024
        ),
        name="layer",
    )(
        block_moves.reshape(1, 512),
        jnp.transpose(kept_blocks[:, 0], (0, 2, 1)),
        kv_cache.reshape(2, 16, 128, 128),
        jnp.transpose(queries[0], (1, 0, 2)),
        new_kv.reshape(4, 2, 128),
        residual.reshape(4, 768),
        expert_ids[0].T,
        gate_weights[0].T,
        norm_gain.reshape(48, 128),
        expert_in.reshape(2, 6144, 256),
        expert_out.reshape(256, 6144),
    )
    return layer.reshape(1, 4, 768), final.reshape(2, 1, 16, 128, 128)


def solution(mesh):
    in_specs = (
        P(None, None, "exp", None),
        P(None, "ctx", None, "exp", None),
        P(None, "exp", "ctx", None, None),
        P(None, "ctx", "exp"),
        P(None, "exp", None, None),
        P(None, "exp", None),
        P(),
        P(),
        P(),
        P("exp", None, None, "ctx"),
        P("exp", "ctx", None),
    )
    out_specs = (P(None, "ctx", "exp"), P(None, "exp", "ctx", None, None))
    return jax.shard_map(
        per_device, mesh=mesh, in_specs=in_specs, out_specs=out_specs, check_vma=False
    )
```

time: 687 us -> 85.7 us (0.12)
  the two profiles are of different devices: /device:TPU:1 before, /device:TPU:2 now
where the time goes in v1:
time: 85.7 us; the launch traced here: 85.5 us
  Pallas kernels  81.3 us (95%)
  local copies, waits for them, and re-layouts  3.6 us (4%)
    pallas_call x1, Pallas kernels, per_device(): pl.pallas_call(kernel, out_shape=(jax.ShapeDtypeStruct((4, 768), BF16), j...  81.3 us
    unnamed x2, local copies, waits for them, and re-layouts  3.6 us

profile of v1, /device:TPU:2, one launch (start us, length us, event | category | flops | bytes accessed | tf_op | source)
XLA Modules:
  0.0 85.5 jit_solution(2960411540038963634)
XLA Ops:
  0.6 81.3 %layer.1 = (bf16[4,768]{1,0:T(4,128)(2,1)}, bf16[2,16,128,128]{3,2,1,0:T(8,128)(2,1)}) custom-call(s32[1,512]{1,0:T(1,128)} %bitcast.32, s32[2,4,128]{2,1,0:T(4,128)} %bitcast.31, bf16[2,16,128,128]{3,2,1,0:T(8,128)(2,1)} %bitcast.25, bf16[6,128,128]{2,1,0:T(8,128)(2,1)} %bitcast.27, bf16[4,2,128]{2,1,0:T(2,128)(2,1)} %bitcast.33, bf16[4,768]{1,0:T(4,128)(2,1)} %bitcast.29, ...), custom_call_target="tpu_custom_call" | custom-call | tf_op jit(solution)/shard_map/layer/pallas_call | solution.py:401
  81.9 1.3 %copy.16 = bf16[1,4,768]{2,1,0:T(4,128)(2,1)} copy(bf16[1,4,768]{2,1,0:T(4,128)(2,1)} %bitcast.30) | data formatting | bytes 12288
  83.2 2.3 %copy.17 = bf16[2,1,16,128,128]{4,3,2,1,0:T(8,128)(2,1)} copy(bf16[2,1,16,128,128]{4,3,2,1,0:T(8,128)(2,1)} %bitcast.26) | data formatting | bytes 2097152

commit v2 on v1

--- a/solution.py
+++ b/solution.py
@@ -13,9 +13,13 @@
 EPS = 1e-05
 F32, BF16, I32 = jnp.float32, jnp.bfloat16, jnp.int32
 
-DZ_ORDER = (4, 3, 5, 2, 6, 1, 7, 0)
-ORDER = tuple((dx, dz) for dz in DZ_ORDER for dx in (2, 1, 3, 0) if (dx, dz) != (0, 0))
-PACE = (0, 4, 4, 4, 8, 8, 3, 0)
+ORDER = tuple(
+    (dx, dz)
+    for dz in (0, 1, 7, 4, 3, 5, 2, 6)
+    for dx in (2, 1, 3, 0)
+    if (dx, dz) != (0, 0)
+)
+PACE = (5, 16, 10, 0, 0, 0, 0)
 
 
 def iota(shape, dim):
@@ -38,9 +42,9 @@
 
 def kernel(
     moves_hbm, kept_hbm, cache_hbm, q_hbm, nkv_hbm, res_hbm, ids_hbm, gates_hbm, gain_hbm, win_hbm, wout_hbm,
-    lay_ref, fin_ref,
-    moves_ref, kept_ref, cache, q_ref, nkv_ref, res_ref, ids_ref, gates_ref, gain_ref, win, wout, idxv, idxs, send_a, recv_a, gx, send_e, recv_e, send_f, recv_f, send_g, recv_g, send_h, recv_h,
-    send_r, recv_r, scr, nks, nvs, slots, gatev, selt, att_s, res_s,
+    lay_ref, recv_r, idxv,
+    moves_ref, kept_ref, cache, q_ref, nkv_ref, res_ref, ids_ref, gates_ref, gain_ref, win, wout, idxs, send_a, recv_a, gx, send_e, recv_e, send_f, recv_f, send_g, recv_g, send_h, recv_h,
+    send_r, scr, nks, nvs, slots, gatev, selt, att_s, res_s,
     lsem, sa, ra, sc, rc, sd, rd, se, re, sf, rf, sg, rg, sh, rh, sr, rr,
 ):
     c = lax.axis_index("ctx")
@@ -110,19 +114,6 @@
     to_smem = pltpu.make_async_copy(idxv, idxs, lsem.at[11])
     to_smem.start()
 
-    loads[2].wait()
-    loads[9].start()
-    loads[10].start()
-    to_smem.wait()
-
-    def pack(o, carry):
-        send_r[o] = cache[:, idxs[0, o]]
-        return carry
-
-    lax.fori_loop(0, 32, pack, 0)
-
-    pl.semaphore_wait(barrier, 38)
-
     def copy_a(o):
         dx, dz = lax.div(o, 8), lax.rem(o, 8)
         t = ctx_at(dx, dz)
@@ -134,9 +125,10 @@
     done = [0]
 
     def relocate(count):
-        for dx, dz in ORDER[done[0] : done[0] + count]:
+        for n in range(done[0], min(done[0] + count, len(ORDER))):
+            dx, dz = ORDER[n]
             copy_r(dx * 8 + dz, dx, dz).start()
-        done[0] += count
+            done[0] = n + 1
 
     def loop(lo, hi, body):
         def step(o, carry):
@@ -144,8 +136,6 @@
             return carry
 
         lax.fori_loop(lo, hi, step, 0)
-
-    relocate(PACE[0])
 
     rsub, rlane = iota((128, 128), 0), iota((128, 128), 1)
     kept0 = kept_ref[0]
@@ -161,6 +151,9 @@
     loads[3].wait()
     heads = [dot(ownb[16 * i : 16 * i + 16], q_ref[i]) for i in range(6)]
     q96 = jnp.concatenate(heads + [jnp.zeros((32, 128), F32)], axis=0).astype(BF16)
+    loads[2].wait()
+    loads[9].start()
+    loads[10].start()
     scores = jnp.zeros((128, 128), F32)
     for j in range(16):
         scores = jnp.where((rsub & 15) == j, dot_nt(q96, cache[0, j]), scores)
@@ -192,9 +185,21 @@
     stat = dot(lift, jnp.concatenate(stats, axis=0)).reshape(32, 8, 128)
     send_a[...] = jnp.concatenate([values[:, 0:24], stat], axis=1).astype(BF16)
 
+    pl.semaphore_wait(barrier, 38)
     loop(1, 32, lambda o: copy_a(o).start())
-    relocate(PACE[1])
     recv_a[0] = send_a[c]
+
+    to_smem.wait()
+
+    def pack(o, carry):
+        send_r[o] = cache[:, idxs[0, o]]
+        return carry
+
+    lax.fori_loop(0, 32, pack, 0)
+
+    relocate(PACE[0])
+    own_block = pltpu.make_async_copy(send_r.at[0], recv_r.at[0], lsem.at[12])
+    own_block.start()
 
     for load in loads[4:9]:
         load.wait()
@@ -267,10 +272,10 @@
         return remote(gx.at[0], gx.at[dx], sd.at[dx], rd.at[dx], ctx=ctx_at(dx, 0))
 
     loop(1, 8, lambda dz: copy_c(dz).start())
-    relocate(PACE[2])
+    relocate(PACE[1])
     loop(1, 8, lambda dz: copy_c(dz).wait_recv())
     loop(1, 4, lambda dx: copy_d(dx).start())
-    relocate(PACE[3])
+    relocate(PACE[2])
     loop(1, 4, lambda dx: copy_d(dx).wait_recv())
 
     flat = gx[...].reshape(32, 32, 128).astype(F32).reshape(16, 2, 32, 128)
@@ -289,7 +294,7 @@
     for j in range(8):
         send_e[j] = dot(sel[64 * j : 64 * j + 64], tokens).astype(BF16)
     loop(1, 8, lambda o: copy_e(o).start())
-    relocate(PACE[4])
+    relocate(PACE[3])
     recv_e[e] = send_e[e]
     loads[9].wait()
 
@@ -332,7 +337,7 @@
         copy_f(o).start()
 
     loop(1, 8, produce)
-    relocate(PACE[5])
+    relocate(PACE[4])
     recv_f[e] = second_half(e)
     loop(1, 8, lambda o: copy_f(o).wait_recv())
     mixed = dot(selt[...], recv_f[...].reshape(512, 768))
@@ -346,7 +351,7 @@
         return remote(send_h.at[dz], recv_h.at[dz], sh.at[dz], rh.at[dz], ctx=ctx_at(0, 8 - dz))
 
     loop(1, 4, lambda dx: copy_g(dx).start())
-    relocate(PACE[6])
+    relocate(PACE[5])
     loop(1, 4, lambda dx: copy_g(dx).wait_recv())
     summed = mixed[0:32] + recv_g[1].astype(F32) + recv_g[2].astype(F32) + recv_g[3].astype(F32)
     cols = [summed[:, 128 * i : 128 * i + 128].reshape(4, 8, 128) for i in range(6)]
@@ -372,15 +377,8 @@
     for i in range(6):
         lay_ref[:, 128 * i : 128 * i + 128] = att_s[4 * i : 4 * i + 4].astype(BF16)
 
-    recv_r[0] = send_r[0]
+    own_block.wait()
     loop(1, 32, lambda o: copy_r(o, lax.div(o, 8), lax.rem(o, 8)).wait_recv())
-
-    def place_block(s):
-        block = recv_r[idxs[1, s]]
-        fin_ref[:, s] = jnp.where(idxs[2, s] > 0, block, jnp.zeros_like(block))
-
-    loop(0, 16, place_block)
-
     loop(1, 32, lambda o: copy_a(o).wait_send())
     loop(1, 8, lambda dz: copy_c(dz).wait_send())
     loop(1, 4, lambda dx: copy_d(dx).wait_send())
@@ -391,6 +389,31 @@
     loop(1, 32, lambda o: copy_r(o, lax.div(o, 8), lax.rem(o, 8)).wait_send())
 
 
+def place_blocks(idxs, layer_hbm, blocks_hbm, lay_hbm, fin_hbm, zeros, sem):
+    last = pltpu.make_async_copy(layer_hbm, lay_hbm, sem.at[16])
+    last.start()
+    zeros[...] = jnp.zeros_like(zeros)
+
+    def start(s, carry):
+        @pl.when(idxs[2, s] > 0)
+        def _():
+            pltpu.make_async_copy(blocks_hbm.at[idxs[1, s]], fin_hbm.at[:, s], sem.at[s]).start()
+
+        @pl.when(idxs[2, s] == 0)
+        def _():
+            pltpu.make_async_copy(zeros, fin_hbm.at[:, s], sem.at[s]).start()
+
+        return carry
+
+    def wait(s, carry):
+        pltpu.make_async_copy(zeros, fin_hbm.at[:, s], sem.at[s]).wait()
+        return carry
+
+    lax.fori_loop(0, 16, start, 0)
+    lax.fori_loop(0, 16, wait, 0)
+    last.wait()
+
+
 def per_device(
     queries, new_kv, kv_cache, residual, kept_blocks, block_moves, expert_ids, gate_weights, norm_gain, expert_in,
     expert_out,
@@ -398,14 +421,15 @@
     vmem = pl.BlockSpec(memory_space=pltpu.VMEM)
     hbm = pl.BlockSpec(memory_space=pl.ANY)
     dma = pltpu.SemaphoreType.DMA
-    layer, final = pl.pallas_call(
+    layer, blocks, index = pl.pallas_call(
         kernel,
         out_shape=(
             jax.ShapeDtypeStruct((4, 768), BF16),
-            jax.ShapeDtypeStruct((2, 16, 128, 128), BF16),
+            jax.ShapeDtypeStruct((32, 2, 128, 128), BF16),
+            jax.ShapeDtypeStruct((8, 128), I32),
         ),
         in_specs=[hbm] * 11,
-        out_specs=(vmem, vmem),
+        out_specs=(vmem, hbm, vmem),
         scratch_shapes=[
             pltpu.VMEM((1, 512), I32),
             pltpu.VMEM((2, 4, 128), I32),
@@ -418,7 +442,6 @@
             pltpu.VMEM((48, 128), F32),
             pltpu.VMEM((2, 6144, 256), BF16),
             pltpu.VMEM((256, 6144), BF16),
-            pltpu.VMEM((8, 128), I32),
             pltpu.SMEM((8, 128), I32),
             pltpu.VMEM((32, 32, 128), BF16),
             pltpu.VMEM((32, 32, 128), BF16),
@@ -432,7 +455,6 @@
             pltpu.VMEM((8, 32, 128), BF16),
             pltpu.VMEM((8, 32, 128), BF16),
             pltpu.VMEM((32, 2, 128, 128), BF16),
-            pltpu.VMEM((32, 2, 128, 128), BF16),
             pltpu.VMEM((8, 128), F32),
             pltpu.VMEM((8, 128), F32),
             pltpu.VMEM((8, 128), F32),
@@ -441,7 +463,7 @@
             pltpu.VMEM((128, 512), BF16),
             pltpu.VMEM((24, 128), F32),
             pltpu.VMEM((24, 128), F32),
-            dma((12,)),
+            dma((13,)),
             dma((32,)), dma((32,)),
             dma((8,)), dma((8,)),
             dma((4,)), dma((4,)),
@@ -468,6 +490,18 @@
         expert_in.reshape(2, 6144, 256),
         expert_out.reshape(256, 6144),
     )
+    layer, final = pl.pallas_call(
+        place_blocks,
+        out_shape=(
+            jax.ShapeDtypeStruct((4, 768), BF16),
+            jax.ShapeDtypeStruct((2, 16, 128, 128), BF16),
+        ),
+        in_specs=[pl.BlockSpec(memory_space=pltpu.SMEM), hbm, hbm],
+        out_specs=(hbm, hbm),
+        scratch_shapes=[pltpu.VMEM((2, 128, 128), BF16), dma((17,))],
+        compiler_params=pltpu.CompilerParams(vmem_limit_bytes=60 * 1024 * 1024),
+        name="place_blocks",
+    )(index, layer, blocks)
     return layer.reshape(1, 4, 768), final.reshape(2, 1, 16, 128, 128)
 
 

time: 85.7 us -> 104 us (1.21)
  the two profiles are of different devices: /device:TPU:2 before, /device:TPU:54 now
where the time goes in v2:
time: 104 us
  Pallas kernels  103 us (99%)
    pallas_call x1, Pallas kernels, per_device(): pl.pallas_call(kernel, out_shape=(jax.ShapeDtypeStruct((4, 768), BF16), j...  71.5 us
    pallas_call x1, Pallas kernels, per_device(): pl.pallas_call(place_blocks, out_shape=(jax.ShapeDtypeStruct((4, 768), BF...  31.9 us

profile of v2, /device:TPU:54, one launch (start us, length us, event | category | flops | bytes accessed | tf_op | source)
XLA Modules:
  0.0 104.0 jit_solution(2049104217892356684)
XLA Ops:
  0.6 71.5 %layer.1 = (bf16[4,768]{1,0:T(4,128)(2,1)}, bf16[32,2,128,128]{3,2,1,0:T(8,128)(2,1)}, s32[8,128]{1,0:T(8,128)}) custom-call(s32[1,512]{1,0:T(1,128)} %bitcast.30, s32[2,4,128]{2,1,0:T(4,128)} %bitcast.29, bf16[2,16,128,128]{3,2,1,0:T(8,128)(2,1)} %bitcast.25, bf16[6,128,128]{2,1,0:T(8,128)(2,1)} %bitcast.26, bf16[4,2,128]{2,1,0:T(2,128)(2,1)} %bitcast.31, ...), custom_call_target="tpu_custom_call" | custom-call | tf_op jit(solution)/shard_map/layer/pallas_call | solution.py:424
  72.1 31.9 %place_blocks.1 = (bf16[4,768]{1,0:T(4,128)(2,1)}, bf16[2,16,128,128]{3,2,1,0:T(8,128)(2,1)}) custom-call(s32[8,128]{1,0:T(8,128)} %get-tuple-element.7.idxs, bf16[4,768]{1,0:T(4,128)(2,1)} %get-tuple-element.8.layer_hbm, bf16[32,2,128,128]{3,2,1,0:T(8,128)(2,1)} %get-tuple-element.9.blocks_hbm), custom_call_target="tpu_custom_call" | custom-call | tf_op jit(solution)/shard_map/place_blocks/pallas_call | solution.py:493

commit v3 on v2

--- a/solution.py
+++ b/solution.py
@@ -13,13 +13,25 @@
 EPS = 1e-05
 F32, BF16, I32 = jnp.float32, jnp.bfloat16, jnp.int32
 
-ORDER = tuple(
-    (dx, dz)
-    for dz in (0, 1, 7, 4, 3, 5, 2, 6)
-    for dx in (2, 1, 3, 0)
-    if (dx, dz) != (0, 0)
+def along_z(*dzs):
+    return tuple((0, dz) for dz in dzs)
+
+
+def mixed_with(*dzs):
+    return tuple((dx, dz) for dz in dzs for dx in (2, 1, 3))
+
+
+ALONG_X = ((2, 0), (1, 0), (3, 0))
+STAGES = (
+    along_z(1, 7),
+    ALONG_X,
+    along_z(2, 6, 3, 5, 4),
+    mixed_with(4, 3, 5),
+    mixed_with(2, 6, 1, 7),
+    (),
+    (),
+    (),
 )
-PACE = (5, 16, 10, 0, 0, 0, 0)
 
 
 def iota(shape, dim):
@@ -43,9 +55,10 @@
 def kernel(
     moves_hbm, kept_hbm, cache_hbm, q_hbm, nkv_hbm, res_hbm, ids_hbm, gates_hbm, gain_hbm, win_hbm, wout_hbm,
     lay_ref, recv_r, idxv,
-    moves_ref, kept_ref, cache, q_ref, nkv_ref, res_ref, ids_ref, gates_ref, gain_ref, win, wout, idxs, send_a, recv_a, gx, send_e, recv_e, send_f, recv_f, send_g, recv_g, send_h, recv_h,
-    send_r, scr, nks, nvs, slots, gatev, selt, att_s, res_s,
-    lsem, sa, ra, sc, rc, sd, rd, se, re, sf, rf, sg, rg, sh, rh, sr, rr,
+    moves_ref, kept_ref, cache, q_ref, nkv_ref, res_ref, ids_ref, gates_ref, gain_ref, win, wout, idxs,
+    send_a, recv_a, send_b, recv_b, gx, send_e, recv_e, send_f, recv_f, send_n, recv_n, send_g, recv_g, send_h, recv_h,
+    send_r, scr, nks, nvs, slots, gatev, sel_far, sel_near, att_s, res_s,
+    lsem, sa, ra, sb, rb, sc, rc, sd, rd, se, re, sf, rf, sn, rn, sg, rg, sh, rh, sr, rr,
 ):
     c = lax.axis_index("ctx")
     e = lax.axis_index("exp")
@@ -114,21 +127,20 @@
     to_smem = pltpu.make_async_copy(idxv, idxs, lsem.at[11])
     to_smem.start()
 
-    def copy_a(o):
-        dx, dz = lax.div(o, 8), lax.rem(o, 8)
-        t = ctx_at(dx, dz)
-        return remote(send_a.at[t], recv_a.at[o], sa.at[o], ra.at[o], ctx=t)
+    def copy_a(dx):
+        row = lax.rem(x + dx, 4)
+        return remote(send_a.at[row], recv_a.at[dx], sa.at[dx], ra.at[dx], ctx=row * 8 + z)
+
+    def copy_b(dz):
+        to = lax.rem(z + dz, 8)
+        return remote(send_b.at[to], recv_b.at[dz], sb.at[dz], rb.at[dz], ctx=x * 8 + to)
 
     def copy_r(o, dx, dz):
         return remote(send_r.at[o], recv_r.at[o], sr.at[o], rr.at[o], ctx=ctx_at(dx, dz))
 
-    done = [0]
-
-    def relocate(count):
-        for n in range(done[0], min(done[0] + count, len(ORDER))):
-            dx, dz = ORDER[n]
+    def relocate(stage):
+        for dx, dz in STAGES[stage]:
             copy_r(dx * 8 + dz, dx, dz).start()
-            done[0] = n + 1
 
     def loop(lo, hi, body):
         def step(o, carry):
@@ -183,11 +195,11 @@
     row256 = iota((256, 128), 0)
     lift = jnp.concatenate([jnp.where(row256 == code + t, 1.0, 0.0).astype(BF16) for t in range(6)], axis=1)
     stat = dot(lift, jnp.concatenate(stats, axis=0)).reshape(32, 8, 128)
-    send_a[...] = jnp.concatenate([values[:, 0:24], stat], axis=1).astype(BF16)
+    send_a[...] = jnp.concatenate([values[:, 0:24], stat], axis=1).astype(BF16).reshape(4, 8, 32, 128)
 
     pl.semaphore_wait(barrier, 38)
-    loop(1, 32, lambda o: copy_a(o).start())
-    recv_a[0] = send_a[c]
+    loop(1, 4, lambda dx: copy_a(dx).start())
+    recv_a[0] = send_a[x]
 
     to_smem.wait()
 
@@ -197,7 +209,7 @@
 
     lax.fori_loop(0, 32, pack, 0)
 
-    relocate(PACE[0])
+    relocate(0)
     own_block = pltpu.make_async_copy(send_r.at[0], recv_r.at[0], lsem.at[12])
     own_block.start()
 
@@ -240,26 +252,57 @@
     gatev[...] = jnp.where(r0 == s8, w0, 0.0) + jnp.where(r1 == s8, w1, 0.0)
     row64 = iota((64, 128), 0)
     sel = jnp.concatenate([jnp.where(row64 == slot[j : j + 1], 1.0, 0.0) for j in range(8)], axis=0)
-    selt[...] = sel.T.astype(BF16)
-    sel = sel.astype(BF16)
+    picks = []
+    for dx in range(4):
+        block = jnp.concatenate([sel[64 * j + 16 * dx : 64 * j + 16 * dx + 16] for j in range(8)], axis=0)
+        if dx:
+            block = pltpu.roll(block, 128 - 32 * dx, 1)
+        picks.append(block[:, 0:32].astype(BF16))
+    far_rows = jnp.concatenate([sel[64 * j + 16 : 64 * j + 64] for j in range(8)], axis=0).T
+    near_rows = jnp.concatenate([sel[64 * j : 64 * j + 16] for j in range(8)], axis=0).T
+    sel_far[...] = far_rows[32:128].astype(BF16)
+    sel_near[...] = near_rows[0:32].astype(BF16)
     gate_col = jnp.sum(
         jnp.where(row64 == slots[pl.ds(e, 1)], gatev[pl.ds(e, 1)], 0.0), axis=1, keepdims=True
     )
 
-    loop(1, 32, lambda o: copy_a(o).wait_recv())
-    got = recv_a[...].astype(F32)
-    st = got[:, 24:32]
-    qi = iota((32, 8, 128), 1)
-    m = jnp.sum(jnp.where(qi < 3, st, 0.0), axis=1, keepdims=True)
-    l = jnp.sum(jnp.where((qi >= 3) & (qi < 6), st, 0.0), axis=1, keepdims=True)
-    m = jnp.where(l > 0, m, NEG)
+    def unpack(got):
+        st = got[:, 24:32]
+        qi = iota(st.shape, 1)
+        m = jnp.sum(jnp.where(qi < 3, st, 0.0), axis=1, keepdims=True)
+        l = jnp.sum(jnp.where((qi >= 3) & (qi < 6), st, 0.0), axis=1, keepdims=True)
+        return jnp.where(l > 0, m, NEG), l
+
+    def column(w):
+        wide = jnp.broadcast_to(w, (w.shape[0], 24, 128))
+        return jnp.sum(jnp.where(eye24[None], wide, 0.0), axis=2, keepdims=True)
+
+    loop(1, 4, lambda dx: copy_a(dx).wait_recv())
+    got = recv_a[...].astype(F32).reshape(32, 32, 128)
+    m, l = unpack(got)
+    m, l = m.reshape(4, 8, 1, 128), l.reshape(4, 8, 1, 128)
+    top = jnp.max(m, axis=0)
+    w = jnp.where(l > 0, jnp.exp(m - top[None]), 0.0)
+    l = jnp.sum(w * l, axis=0)
+    parts = split3(jnp.where(l > 0, top, 0.0)) + split3(l)
+    qi = iota((8, 8, 128), 1)
+    stat = jnp.zeros((8, 8, 128), F32)
+    for n in range(6):
+        stat = jnp.where(qi == n, parts[n], stat)
+    values = column(w.reshape(32, 1, 128)) * got[:, 0:24]
+    values = jnp.sum(values.reshape(4, 8, 24, 128), axis=0)
+    send_b[...] = jnp.concatenate([values, stat], axis=1).astype(BF16)
+    loop(1, 8, lambda dz: copy_b(dz).start())
+    recv_b[0] = send_b[z]
+    relocate(1)
+    loop(1, 8, lambda dz: copy_b(dz).wait_recv())
+    got = recv_b[...].astype(F32)
+    m, l = unpack(got)
     top = jnp.maximum(jnp.max(m, axis=0), own_score)
     w = jnp.where(l > 0, jnp.exp(m - top[None]), 0.0)
     fresh = jnp.exp(own_score - top)
     inv_den = 1.0 / (jnp.sum(w * l, axis=0) + fresh)
-    w = w * inv_den[None]
-    wcol = jnp.sum(jnp.where(eye24[None], jnp.broadcast_to(w, (32, 24, 128)), 0.0), axis=2, keepdims=True)
-    att = jnp.sum(wcol * got[:, 0:24], axis=0)
+    att = jnp.sum(column(w * inv_den[None]) * got[:, 0:24], axis=0)
     fcol = jnp.sum(jnp.where(eye24, fresh * inv_den, 0.0), axis=1, keepdims=True)
     att = att + fcol * nv24
     hidden = (res_s[...] + att).astype(BF16).astype(F32)
@@ -271,30 +314,34 @@
     def copy_d(dx):
         return remote(gx.at[0], gx.at[dx], sd.at[dx], rd.at[dx], ctx=ctx_at(dx, 0))
 
+    def copy_e(dx, o):
+        t = exp_at(lax.div(o, 2), lax.rem(o, 2))
+        rows = pl.ds(16 * dx, 16)
+        return remote(send_e.at[t, rows], recv_e.at[e, rows], se.at[8 * dx + o], re.at[8 * dx + o], exp=t)
+
+    def dispatch(dx):
+        flat = gx[dx].astype(F32).reshape(4, 2, 32, 128)
+        parts = []
+        for p in range(3):
+            one, two = flat[:, 0, 8 * p : 8 * p + 8], flat[:, 1, 8 * p : 8 * p + 8]
+            parts.append(jnp.where(sub4 < 4, one, pltpu.roll(two, 4, 1)).reshape(32, 128).astype(BF16))
+            parts.append(jnp.where(sub4 < 4, pltpu.roll(one, 4, 1), two).reshape(32, 128).astype(BF16))
+        rows = dot(picks[dx], jnp.concatenate(parts, axis=1)).astype(BF16)
+        for j in range(8):
+            send_e[j, 16 * dx : 16 * dx + 16] = rows[16 * j : 16 * j + 16]
+        loop(1, 8, lambda o: copy_e(dx, o).start())
+
+    sub4 = iota((4, 8, 128), 1)
     loop(1, 8, lambda dz: copy_c(dz).start())
-    relocate(PACE[1])
+    relocate(2)
     loop(1, 8, lambda dz: copy_c(dz).wait_recv())
     loop(1, 4, lambda dx: copy_d(dx).start())
-    relocate(PACE[2])
-    loop(1, 4, lambda dx: copy_d(dx).wait_recv())
-
-    flat = gx[...].reshape(32, 32, 128).astype(F32).reshape(16, 2, 32, 128)
-    sub16 = iota((16, 8, 128), 1)
-    parts = []
-    for p in range(3):
-        one, two = flat[:, 0, 8 * p : 8 * p + 8], flat[:, 1, 8 * p : 8 * p + 8]
-        parts.append(jnp.where(sub16 < 4, one, pltpu.roll(two, 4, 1)).reshape(128, 128).astype(BF16))
-        parts.append(jnp.where(sub16 < 4, pltpu.roll(one, 4, 1), two).reshape(128, 128).astype(BF16))
-    tokens = jnp.concatenate(parts, axis=1)
-
-    def copy_e(o):
-        t = exp_at(lax.div(o, 2), lax.rem(o, 2))
-        return remote(send_e.at[t], recv_e.at[e], se.at[o], re.at[o], exp=t)
-
-    for j in range(8):
-        send_e[j] = dot(sel[64 * j : 64 * j + 64], tokens).astype(BF16)
-    loop(1, 8, lambda o: copy_e(o).start())
-    relocate(PACE[3])
+    dispatch(0)
+    relocate(3)
+    for dx in (1, 3, 2):
+        copy_d(dx).wait_recv()
+        dispatch(dx)
+    relocate(4)
     recv_e[e] = send_e[e]
     loads[9].wait()
 
@@ -311,7 +358,8 @@
         return gate, upper, square
 
     def arrived(o, carry):
-        copy_e(o).wait_recv()
+        for dx in (0, 1, 3, 2):
+            copy_e(dx, o).wait_recv()
         return first_half(o, carry)
 
     zero = jnp.zeros((64, 256), F32)
@@ -326,6 +374,10 @@
         t = exp_at(lax.div(o, 2), lax.rem(o, 2))
         return remote(send_f.at[t], recv_f.at[e], sf.at[o], rf.at[o], exp=t)
 
+    def copy_n(o):
+        t = exp_at(lax.div(o, 2), lax.rem(o, 2))
+        return remote(send_n.at[t], recv_n.at[e], sn.at[o], rn.at[o], exp=t)
+
     def second_half(t):
         start = pl.multiple_of(t * 768, 768)
         return (dot(act, wout[:, pl.ds(start, 768)]) * gate_col).astype(BF16)
@@ -333,16 +385,21 @@
     def produce(n):
         o = 8 - n
         t = exp_at(lax.div(o, 2), lax.rem(o, 2))
-        send_f[t] = second_half(t)
+        rows = second_half(t)
+        send_f[t] = rows[16:64]
+        send_n[t] = rows[0:16]
         copy_f(o).start()
 
     loop(1, 8, produce)
-    relocate(PACE[4])
-    recv_f[e] = second_half(e)
+    loop(1, 8, lambda o: copy_n(o).start())
+    relocate(5)
+    rows = second_half(e)
+    recv_f[e] = rows[16:64]
+    recv_n[e] = rows[0:16]
     loop(1, 8, lambda o: copy_f(o).wait_recv())
-    mixed = dot(selt[...], recv_f[...].reshape(512, 768))
+    mixed = dot(sel_far[...], recv_f[...].reshape(384, 768))
     for dx in range(1, 4):
-        send_g[dx] = mixed[32 * dx : 32 * dx + 32].astype(BF16)
+        send_g[dx] = mixed[32 * dx - 32 : 32 * dx].astype(BF16)
 
     def copy_g(dx):
         return remote(send_g.at[dx], recv_g.at[dx], sg.at[dx], rg.at[dx], ctx=ctx_at(4 - dx, 0))
@@ -351,11 +408,12 @@
         return remote(send_h.at[dz], recv_h.at[dz], sh.at[dz], rh.at[dz], ctx=ctx_at(0, 8 - dz))
 
     loop(1, 4, lambda dx: copy_g(dx).start())
-    relocate(PACE[5])
+    loop(1, 8, lambda o: copy_n(o).wait_recv())
+    mixed = dot(sel_near[...], recv_n[...].reshape(128, 768))
+    relocate(6)
     loop(1, 4, lambda dx: copy_g(dx).wait_recv())
-    summed = mixed[0:32] + recv_g[1].astype(F32) + recv_g[2].astype(F32) + recv_g[3].astype(F32)
+    summed = mixed + recv_g[1].astype(F32) + recv_g[2].astype(F32) + recv_g[3].astype(F32)
     cols = [summed[:, 128 * i : 128 * i + 128].reshape(4, 8, 128) for i in range(6)]
-    sub4 = iota((4, 8, 128), 1)
     evens, odds = [], []
     for p in range(3):
         one, two = cols[2 * p], cols[2 * p + 1]
@@ -367,7 +425,7 @@
         send_h[2 * n] = evens[n].astype(BF16)
         send_h[2 * n + 1] = odds[n].astype(BF16)
     loop(1, 8, lambda dz: copy_h(dz).start())
-    relocate(31)
+    relocate(7)
 
     loop(1, 8, lambda dz: copy_h(dz).wait_recv())
     total = hidden + evens[0, 0:24]
@@ -379,39 +437,58 @@
 
     own_block.wait()
     loop(1, 32, lambda o: copy_r(o, lax.div(o, 8), lax.rem(o, 8)).wait_recv())
-    loop(1, 32, lambda o: copy_a(o).wait_send())
+    loop(1, 4, lambda dx: copy_a(dx).wait_send())
+    loop(1, 8, lambda dz: copy_b(dz).wait_send())
     loop(1, 8, lambda dz: copy_c(dz).wait_send())
     loop(1, 4, lambda dx: copy_d(dx).wait_send())
-    loop(1, 8, lambda o: copy_e(o).wait_send())
+    for dx in range(4):
+        loop(1, 8, lambda o, dx=dx: copy_e(dx, o).wait_send())
     loop(1, 8, lambda o: copy_f(o).wait_send())
+    loop(1, 8, lambda o: copy_n(o).wait_send())
     loop(1, 4, lambda dx: copy_g(dx).wait_send())
     loop(1, 8, lambda dz: copy_h(dz).wait_send())
     loop(1, 32, lambda o: copy_r(o, lax.div(o, 8), lax.rem(o, 8)).wait_send())
 
 
-def place_blocks(idxs, layer_hbm, blocks_hbm, lay_hbm, fin_hbm, zeros, sem):
-    last = pltpu.make_async_copy(layer_hbm, lay_hbm, sem.at[16])
-    last.start()
-    zeros[...] = jnp.zeros_like(zeros)
+def place_blocks(idxs, layer_ref, blocks_hbm, lay_ref, fin_hbm, held, came, went):
+    def load(s):
+        return pltpu.make_async_copy(blocks_hbm.at[idxs[1, s]], held.at[s], came.at[s])
+
+    def store(s):
+        return pltpu.make_async_copy(held.at[s], fin_hbm.at[:, s], went.at[s])
 
     def start(s, carry):
         @pl.when(idxs[2, s] > 0)
         def _():
-            pltpu.make_async_copy(blocks_hbm.at[idxs[1, s]], fin_hbm.at[:, s], sem.at[s]).start()
-
+            load(s).start()
+
+        return carry
+
+    def clear(s, carry):
         @pl.when(idxs[2, s] == 0)
         def _():
-            pltpu.make_async_copy(zeros, fin_hbm.at[:, s], sem.at[s]).start()
+            held[s] = jnp.zeros((2, 128, 128), BF16)
+            store(s).start()
 
         return carry
 
-    def wait(s, carry):
-        pltpu.make_async_copy(zeros, fin_hbm.at[:, s], sem.at[s]).wait()
+    def forward(s, carry):
+        @pl.when(idxs[2, s] > 0)
+        def _():
+            load(s).wait()
+            store(s).start()
+
         return carry
 
+    def finish(s, carry):
+        store(s).wait()
+        return carry
+
     lax.fori_loop(0, 16, start, 0)
-    lax.fori_loop(0, 16, wait, 0)
-    last.wait()
+    lay_ref[...] = layer_ref[...]
+    lax.fori_loop(0, 16, clear, 0)
+    lax.fori_loop(0, 16, forward, 0)
+    lax.fori_loop(0, 16, finish, 0)
 
 
 def per_device(
@@ -443,13 +520,17 @@
             pltpu.VMEM((2, 6144, 256), BF16),
             pltpu.VMEM((256, 6144), BF16),
             pltpu.SMEM((8, 128), I32),
-            pltpu.VMEM((32, 32, 128), BF16),
-            pltpu.VMEM((32, 32, 128), BF16),
+            pltpu.VMEM((4, 8, 32, 128), BF16),
+            pltpu.VMEM((4, 8, 32, 128), BF16),
+            pltpu.VMEM((8, 32, 128), BF16),
+            pltpu.VMEM((8, 32, 128), BF16),
             pltpu.VMEM((4, 8, 32, 128), BF16),
             pltpu.VMEM((8, 64, 768), BF16),
             pltpu.VMEM((8, 64, 768), BF16),
-            pltpu.VMEM((8, 64, 768), BF16),
-            pltpu.VMEM((8, 64, 768), BF16),
+            pltpu.VMEM((8, 48, 768), BF16),
+            pltpu.VMEM((8, 48, 768), BF16),
+            pltpu.VMEM((8, 16, 768), BF16),
+            pltpu.VMEM((8, 16, 768), BF16),
             pltpu.VMEM((4, 32, 768), BF16),
             pltpu.VMEM((4, 32, 768), BF16),
             pltpu.VMEM((8, 32, 128), BF16),
@@ -460,13 +541,16 @@
             pltpu.VMEM((8, 128), F32),
             pltpu.VMEM((8, 128), I32),
             pltpu.VMEM((8, 128), F32),
-            pltpu.VMEM((128, 512), BF16),
+            pltpu.VMEM((96, 384), BF16),
+            pltpu.VMEM((32, 128), BF16),
             pltpu.VMEM((24, 128), F32),
             pltpu.VMEM((24, 128), F32),
             dma((13,)),
-            dma((32,)), dma((32,)),
+            dma((4,)), dma((4,)),
+            dma((8,)), dma((8,)),
             dma((8,)), dma((8,)),
             dma((4,)), dma((4,)),
+            dma((32,)), dma((32,)),
             dma((8,)), dma((8,)),
             dma((8,)), dma((8,)),
             dma((4,)), dma((4,)),
@@ -496,9 +580,9 @@
             jax.ShapeDtypeStruct((4, 768), BF16),
             jax.ShapeDtypeStruct((2, 16, 128, 128), BF16),
         ),
-        in_specs=[pl.BlockSpec(memory_space=pltpu.SMEM), hbm, hbm],
-        out_specs=(hbm, hbm),
-        scratch_shapes=[pltpu.VMEM((2, 128, 128), BF16), dma((17,))],
+        in_specs=[pl.BlockSpec(memory_space=pltpu.SMEM), vmem, hbm],
+        out_specs=(vmem, hbm),
+        scratch_shapes=[pltpu.VMEM((16, 2, 128, 128), BF16), dma((16,)), dma((16,))],
         compiler_params=pltpu.CompilerParams(vmem_limit_bytes=60 * 1024 * 1024),
         name="place_blocks",
     )(index, layer, blocks)

time: 104 us -> 76.1 us (0.73)
  the two profiles are of different devices: /device:TPU:54 before, /device:TPU:1 now
where the time goes in v3:
time: 76.1 us; the launch traced here: 75.9 us
  Pallas kernels  75.2 us (99%)
    pallas_call x1, Pallas kernels, per_device(): pl.pallas_call(kernel, out_shape=(jax.ShapeDtypeStruct((4, 768), BF16), j...  71.9 us
    pallas_call x1, Pallas kernels, per_device(): pl.pallas_call(place_blocks, out_shape=(jax.ShapeDtypeStruct((4, 768), BF...  3.39 us

profile of v3, /device:TPU:1, one launch (start us, length us, event | category | flops | bytes accessed | tf_op | source)
XLA Modules:
  0.0 75.9 jit_solution(14214387310261229243)
XLA Ops:
  0.6 71.9 %layer.1 = (bf16[4,768]{1,0:T(4,128)(2,1)}, bf16[32,2,128,128]{3,2,1,0:T(8,128)(2,1)}, s32[8,128]{1,0:T(8,128)}) custom-call(s32[1,512]{1,0:T(1,128)} %bitcast.30, s32[2,4,128]{2,1,0:T(4,128)} %bitcast.29, bf16[2,16,128,128]{3,2,1,0:T(8,128)(2,1)} %bitcast.25, bf16[6,128,128]{2,1,0:T(8,128)(2,1)} %bitcast.26, bf16[4,2,128]{2,1,0:T(2,128)(2,1)} %bitcast.31, ...), custom_call_target="tpu_custom_call" | custom-call | tf_op jit(solution)/shard_map/layer/pallas_call | solution.py:501
  72.5 3.4 %place_blocks.1 = (bf16[4,768]{1,0:T(4,128)(2,1)}, bf16[2,16,128,128]{3,2,1,0:T(8,128)(2,1)}) custom-call(s32[8,128]{1,0:T(8,128)} %get-tuple-element.7.idxs, bf16[4,768]{1,0:T(4,128)(2,1)} %get-tuple-element.8.layer_ref, bf16[32,2,128,128]{3,2,1,0:T(8,128)(2,1)} %get-tuple-element.9.blocks_hbm), custom_call_target="tpu_custom_call" | custom-call | tf_op jit(solution)/shard_map/place_blocks/pallas_call | solution.py:577

commit v4 on v3

--- a/solution.py
+++ b/solution.py
@@ -23,11 +23,11 @@
 
 ALONG_X = ((2, 0), (1, 0), (3, 0))
 STAGES = (
-    along_z(1, 7),
+    along_z(1, 7, 2, 6),
     ALONG_X,
-    along_z(2, 6, 3, 5, 4),
+    along_z(3, 5, 4) + mixed_with(1),
     mixed_with(4, 3, 5),
-    mixed_with(2, 6, 1, 7),
+    mixed_with(2, 6, 7),
     (),
     (),
     (),

time: 76.1 us -> 74.1 us (0.974)
  Pallas kernels: 75.2 us -> 73.2 us
    pallas_call x1, Pallas kernels: 71.9 us -> 69.7 us  [per_device(): pl.pallas_call(kernel, out_shape=(jax.ShapeDtypeStruct((4, 768), BF16), j...]
where the time goes in v4:
time: 74.1 us; the launch traced here: 73.8 us
  Pallas kernels  73.2 us (99%)
    pallas_call x1, Pallas kernels, per_device(): pl.pallas_call(kernel, out_shape=(jax.ShapeDtypeStruct((4, 768), BF16), j...  69.7 us
    pallas_call x1, Pallas kernels, per_device(): pl.pallas_call(place_blocks, out_shape=(jax.ShapeDtypeStruct((4, 768), BF...  3.45 us

profile of v4, /device:TPU:1, one launch (start us, length us, event | category | flops | bytes accessed | tf_op | source)
XLA Modules:
  0.0 73.8 jit_solution(13551085190474005544)
XLA Ops:
  0.6 69.7 %layer.1 = (bf16[4,768]{1,0:T(4,128)(2,1)}, bf16[32,2,128,128]{3,2,1,0:T(8,128)(2,1)}, s32[8,128]{1,0:T(8,128)}) custom-call(s32[1,512]{1,0:T(1,128)} %bitcast.30, s32[2,4,128]{2,1,0:T(4,128)} %bitcast.29, bf16[2,16,128,128]{3,2,1,0:T(8,128)(2,1)} %bitcast.25, bf16[6,128,128]{2,1,0:T(8,128)(2,1)} %bitcast.26, bf16[4,2,128]{2,1,0:T(2,128)(2,1)} %bitcast.31, ...), custom_call_target="tpu_custom_call" | custom-call | tf_op jit(solution)/shard_map/layer/pallas_call | solution.py:501
  70.4 3.5 %place_blocks.1 = (bf16[4,768]{1,0:T(4,128)(2,1)}, bf16[2,16,128,128]{3,2,1,0:T(8,128)(2,1)}) custom-call(s32[8,128]{1,0:T(8,128)} %get-tuple-element.7.idxs, bf16[4,768]{1,0:T(4,128)(2,1)} %get-tuple-element.8.layer_ref, bf16[32,2,128,128]{3,2,1,0:T(8,128)(2,1)} %get-tuple-element.9.blocks_hbm), custom_call_target="tpu_custom_call" | custom-call | tf_op jit(solution)/shard_map/place_blocks/pallas_call | solution.py:577

commit v5 on v4

--- a/solution.py
+++ b/solution.py
@@ -25,9 +25,9 @@
 STAGES = (
     along_z(1, 7, 2, 6),
     ALONG_X,
-    along_z(3, 5, 4) + mixed_with(1),
+    along_z(3, 5, 4) + mixed_with(1, 7),
     mixed_with(4, 3, 5),
-    mixed_with(2, 6, 7),
+    mixed_with(2, 6),
     (),
     (),
     (),

time: 74.1 us -> 74.7 us (level)
  no operation moved by 1% of the time
where the time goes in v5:
time: 74.7 us; the launch traced here: 74.6 us
  Pallas kernels  73.9 us (99%)
    pallas_call x1, Pallas kernels, per_device(): pl.pallas_call(kernel, out_shape=(jax.ShapeDtypeStruct((4, 768), BF16), j...  70.4 us
    pallas_call x1, Pallas kernels, per_device(): pl.pallas_call(place_blocks, out_shape=(jax.ShapeDtypeStruct((4, 768), BF...  3.5 us

profile of v5, /device:TPU:1, one launch (start us, length us, event | category | flops | bytes accessed | tf_op | source)
XLA Modules:
  0.0 74.6 jit_solution(2347093058063532264)
XLA Ops:
  0.6 70.4 %layer.1 = (bf16[4,768]{1,0:T(4,128)(2,1)}, bf16[32,2,128,128]{3,2,1,0:T(8,128)(2,1)}, s32[8,128]{1,0:T(8,128)}) custom-call(s32[1,512]{1,0:T(1,128)} %bitcast.30, s32[2,4,128]{2,1,0:T(4,128)} %bitcast.29, bf16[2,16,128,128]{3,2,1,0:T(8,128)(2,1)} %bitcast.25, bf16[6,128,128]{2,1,0:T(8,128)(2,1)} %bitcast.26, bf16[4,2,128]{2,1,0:T(2,128)(2,1)} %bitcast.31, ...), custom_call_target="tpu_custom_call" | custom-call | tf_op jit(solution)/shard_map/layer/pallas_call | solution.py:501
  71.1 3.5 %place_blocks.1 = (bf16[4,768]{1,0:T(4,128)(2,1)}, bf16[2,16,128,128]{3,2,1,0:T(8,128)(2,1)}) custom-call(s32[8,128]{1,0:T(8,128)} %get-tuple-element.7.idxs, bf16[4,768]{1,0:T(4,128)(2,1)} %get-tuple-element.8.layer_ref, bf16[32,2,128,128]{3,2,1,0:T(8,128)(2,1)} %get-tuple-element.9.blocks_hbm), custom_call_target="tpu_custom_call" | custom-call | tf_op jit(solution)/shard_map/place_blocks/pallas_call | solution.py:577
